TPU v7x, 256 devices: a whole 4x4x8 slice. The times are simulated.
256 devices in a mesh: particle: 32 (over z_hi, x, core), tile: 8 (over z_lo, y).
Axes of the slice: x: 4, y: 4, z: 8 (z_hi: 4, z_lo: 2; z = z_hi * 2 + z_lo), core: 2. Of those that a mesh axis runs over, the one named last changes fastest.
Arguments:
- ensemble: float32 [32, 4, 128, 2048], P('particle', None, 'tile'), may hold values from -6 to 6
- ancestor: int32 [32], replicated, may hold values from 0 to 31
- velocity: float32 [2, 4, 128, 2048], P(None, None, 'tile'), may hold values from -0.3 to 0.3
- observed: float32 [4, 128, 2048], P(None, 'tile'), may hold values from -6 to 6
- nudge_gain: float32 [4, 128, 2048], P(None, 'tile'), may hold values from 0.05 to 0.3
- forcing: float32 [32, 4, 128, 2048], P('particle', None, 'tile'), may hold values from -4 to 4
Outputs:
- forecast: float32 [32, 4, 128, 2048], P('particle', None, 'tile')
All inputs are finite; a program needn't handle non-finite values.
Results may differ from a plain program's by a relative error of at most 0.00002.
Values sent between devices are 32-bit elements; how exact they have to be, the bound alone decides.
A program may use at most 64 MiB of HBM per device.

v0:
```python
import jax
import jax.numpy as jnp
from jax import lax
from jax.sharding import PartitionSpec as P

ITERS = 3


def padded_2(cells, sides, width):
    for axis, dim in sides:
        count = lax.axis_size(axis)
        ends = count - 1
        head = lax.slice_in_dim(cells, 0, width, axis=dim)
        tail = lax.slice_in_dim(cells, cells.shape[dim] - width, cells.shape[dim], axis=dim)
        cells = jnp.concatenate(
            [
                lax.ppermute(tail, axis, [(i, (i + 1) % count) for i in range(ends)]),
                cells,
                lax.ppermute(head, axis, [((i + 1) % count, i) for i in range(ends)]),
            ],
            axis=dim,
        )
    return cells


def step_strip(field, cross, along, observed, nudge_gain, forcing):
    rows = field.shape[2]
    padded = padded_2(field, (("tile", 2),), 2)
    dy = (
        8.0 * (padded[:, :, 3 : rows + 3] - padded[:, :, 1 : rows + 1])
        - (padded[:, :, 4 : rows + 4] - padded[:, :, 0:rows])
    ) / 12.0
    east = jnp.roll(field, -1, 3)
    west = jnp.roll(field, 1, 3)
    dx = (8.0 * (east - west) - (jnp.roll(field, -2, 3) - jnp.roll(field, 2, 3))) / 12.0
    lap = padded[:, :, 3 : rows + 3] + padded[:, :, 1 : rows + 1] + east + west - 4.0 * field
    upper = jnp.concatenate([field[:, 1:], field[:, -1:]], axis=1)
    lower = jnp.concatenate([field[:, :1], field[:, :-1]], axis=1)
    vmix = upper + lower - 2.0 * field
    return (
        field
        - cross * dx
        - along * dy
        + 0.1 * lap
        + 0.1 * vmix
        + nudge_gain * (observed - field)
        + forcing
    )


def lax_slice(values, first, count):
    return jax.lax.dynamic_slice_in_dim(values, first, count, 0)


def shards(ensemble, ancestor, velocity, observed, nudge_gain, forcing):
    local_count, levels, strip_rows, columns_all = ensemble.shape
    first = lax.axis_index("particle") * local_count
    wanted = lax_slice(ancestor, first, local_count)
    piece = lax.all_gather(ensemble, "particle", axis=0, tiled=True)
    count = piece.shape[0]
    inside = (wanted >= 0) & (wanted < count)
    picked = jnp.take(piece, jnp.clip(wanted, 0, count - 1), axis=0)
    field = jnp.where(inside[:, None, None, None], picked, jnp.zeros_like(ensemble))
    for step in range(ITERS):
        field = step_strip(field, velocity[0], velocity[1], observed, nudge_gain, forcing)
    return field


def solution(mesh):
    placed = (
        P("particle", None, "tile", None),
        P(),
        P(None, None, "tile", None),
        P(None, "tile", None),
        P(None, "tile", None),
        P("particle", None, "tile", None),
    )
    return jax.shard_map(
        shards,
        mesh=mesh,
        in_specs=placed,
        out_specs=P("particle", None, "tile", None),
        check_vma=False,
    )
```

profile of v0, /device:TPU:32, one launch (start us, length us, event | category | flops | bytes accessed | tf_op | source)
XLA Modules:
  0.0 176.5 jit_solution(15899788364277640432)
XLA Ops:
  6.5 0.0 copy-start.1
  6.5 0.0 copy-start.2
  6.5 0.0 copy-start.3
  6.5 0.0 copy-start
  6.5 0.0 all-gather.2.cloned.1.call-start
  6.6 0.7 all-gather.2.cloned.1.call-update
  7.3 1.3 dynamic_slice.3
  10.5 120.4 %all-gather.2.cloned.1.call-done = f32[32,4,16,2048]{3,2,1,0:T(8,128)} async-done(((f32[1,4,16,2048]{3,2,1,0:T(8,128)}), f32[32,4,16,2048]{3,2,1,0:T(8,128)}) %all-gather.2.cloned.1.call-update) | async-done | bytes 16777232 | tf_op jit(solution)/shard_map/all_gather | solution.py:59
  130.9 1.1 fusion.54
  132.0 0.1 fusion.73
  132.2 0.1 fusion.72
  132.2 0.2 fusion.74
  132.4 0.2 fusion.69
  132.7 1.9 %collective-permute-start = (f32[1,4,2,2048]{3,2,1,0:T(2,128)S(1)}, f32[1,4,2,2048]{3,2,1,0:T(2,128)S(1)}, u32[]{:S(2)}, u32[]{:S(2)}) collective-permute-start(f32[1,4,2,2048]{3,2,1,0:T(2,128)S(1)} %get-tuple-element.56), channel_id=1, source_target_pairs={{1,0},{2,1},{3,2},{4,3},{5,4},{6,5},{7,6},{9,8},{10,9},{11,10},{12... | collective-permute-start | bytes 196616 | tf_op jit(solution)/shard_map/ppermute | solution.py:19
  134.6 3.9 %collective-permute-start.1 = (f32[1,4,2,2048]{3,2,1,0:T(2,128)S(1)}, f32[1,4,2,2048]{3,2,1,0:T(2,128)S(1)}, u32[]{:S(2)}, u32[]{:S(2)}) collective-permute-start(f32[1,4,2,2048]{3,2,1,0:T(2,128)S(1)} %get-tuple-element.57), channel_id=1, source_target_pairs={{0,1},{1,2},{2,3},{3,4},{4,5},{5,6},{6,7},{8,9},{9,10},{10,11},{11... | collective-permute-start | bytes 196616 | tf_op jit(solution)/shard_map/ppermute | solution.py:17
  138.5 0.1 fusion.70
  138.6 0.2 collective-permute-done
  138.8 4.0 %collective-permute-done.1 = f32[1,4,2,2048]{3,2,1,0:T(2,128)S(1)} collective-permute-done((f32[1,4,2,2048]{3,2,1,0:T(2,128)S(1)}, f32[1,4,2,2048]{3,2,1,0:T(2,128)S(1)}, u32[]{:S(2)}, u32[]{:S(2)}) %collective-permute-start.1) | collective-permute-done | bytes 65568 | tf_op jit(solution)/shard_map/ppermute | solution.py:17
  142.8 2.5 %fusion.32 = f32[1,4,16,2048]{3,2,1,0:T(8,128)S(1)} fusion(f32[1,4,16,2048]{3,2,1,0:T(8,128)} %param.11, f32[1,4,16,2048]{3,2,1,0:T(8,128)S(1)} %fusion.54, f32[1,4,2,2048]{3,2,1,0:T(2,128)S(1)} %collective-permute-done.1, f32[1,4,2,2048]{3,2,1,0:T(2,128)S(1)} %collective-permute-done, f32[1,4,16,2]{3,2,1,0:T(8,128)S(1)} %get-tuple-element.53, ...), kind=kLoop, calls=%fused_computation.49 | loop fusion | flops 5242880 | bytes 6946816 | tf_op jit(solution)/shard_map/add | solution.py:41
  145.4 0.1 fusion.66
  145.5 0.1 fusion.65
  145.6 0.2 fusion.67
  145.8 0.2 fusion.62
  146.0 1.9 %collective-permute-start.2 = (f32[1,4,2,2048]{3,2,1,0:T(2,128)S(1)}, f32[1,4,2,2048]{3,2,1,0:T(2,128)S(1)}, u32[]{:S(2)}, u32[]{:S(2)}) collective-permute-start(f32[1,4,2,2048]{3,2,1,0:T(2,128)S(1)} %get-tuple-element.42), channel_id=1, source_target_pairs={{1,0},{2,1},{3,2},{4,3},{5,4},{6,5},{7,6},{9,8},{10,9},{11,10},{12... | collective-permute-start | bytes 196616 | tf_op jit(solution)/shard_map/ppermute | solution.py:19
  148.0 3.9 %collective-permute-start.3 = (f32[1,4,2,2048]{3,2,1,0:T(2,128)S(1)}, f32[1,4,2,2048]{3,2,1,0:T(2,128)S(1)}, u32[]{:S(2)}, u32[]{:S(2)}) collective-permute-start(f32[1,4,2,2048]{3,2,1,0:T(2,128)S(1)} %get-tuple-element.43), channel_id=1, source_target_pairs={{0,1},{1,2},{2,3},{3,4},{4,5},{5,6},{6,7},{8,9},{9,10},{10,11},{11... | collective-permute-start | bytes 196616 | tf_op jit(solution)/shard_map/ppermute | solution.py:17
  151.9 0.1 fusion.63
  152.0 0.2 collective-permute-done.2
  152.2 4.0 %collective-permute-done.3 = f32[1,4,2,2048]{3,2,1,0:T(2,128)S(1)} collective-permute-done((f32[1,4,2,2048]{3,2,1,0:T(2,128)S(1)}, f32[1,4,2,2048]{3,2,1,0:T(2,128)S(1)}, u32[]{:S(2)}, u32[]{:S(2)}) %collective-permute-start.3) | collective-permute-done | bytes 65568 | tf_op jit(solution)/shard_map/ppermute | solution.py:17
  156.2 0.0 copy-done.1
  156.2 0.0 copy-done.2
  156.2 0.0 copy-done.3
  156.2 0.0 copy-done
  156.2 0.9 fusion.23
  157.1 0.1 fusion.59
  157.3 0.1 fusion.58
  157.4 0.2 fusion.60
  157.6 0.2 fusion.55
  157.8 1.9 %collective-permute-start.4 = (f32[1,4,2,2048]{3,2,1,0:T(2,128)S(1)}, f32[1,4,2,2048]{3,2,1,0:T(2,128)S(1)}, u32[]{:S(2)}, u32[]{:S(2)}) collective-permute-start(f32[1,4,2,2048]{3,2,1,0:T(2,128)S(1)} %get-tuple-element.28), channel_id=1, source_target_pairs={{1,0},{2,1},{3,2},{4,3},{5,4},{6,5},{7,6},{9,8},{10,9},{11,10},{12... | collective-permute-start | bytes 196616 | tf_op jit(solution)/shard_map/ppermute | solution.py:19
  159.7 3.9 %collective-permute-start.5 = (f32[1,4,2,2048]{3,2,1,0:T(2,128)S(1)}, f32[1,4,2,2048]{3,2,1,0:T(2,128)S(1)}, u32[]{:S(2)}, u32[]{:S(2)}) collective-permute-start(f32[1,4,2,2048]{3,2,1,0:T(2,128)S(1)} %get-tuple-element.29), channel_id=1, source_target_pairs={{0,1},{1,2},{2,3},{3,4},{4,5},{5,6},{6,7},{8,9},{9,10},{10,11},{11... | collective-permute-start | bytes 196616 | tf_op jit(solution)/shard_map/ppermute | solution.py:17
  163.6 0.1 fusion.56
  163.7 0.2 collective-permute-done.4
  163.9 4.0 %collective-permute-done.5 = f32[1,4,2,2048]{3,2,1,0:T(2,128)S(1)} collective-permute-done((f32[1,4,2,2048]{3,2,1,0:T(2,128)S(1)}, f32[1,4,2,2048]{3,2,1,0:T(2,128)S(1)}, u32[]{:S(2)}, u32[]{:S(2)}) %collective-permute-start.5) | collective-permute-done | bytes 65568 | tf_op jit(solution)/shard_map/ppermute | solution.py:17
  168.0 1.7 fusion.14
  (6 shorter events, 0.2 us)
Async XLA Ops:
  6.5 149.7 %copy-start.1 = (f32[1,4,16,2048]{3,2,1,0:T(8,128)S(1)}, f32[1,4,16,2048]{3,2,1,0:T(8,128)}, u32[]{:S(2)}) copy-start(f32[1,4,16,2048]{3,2,1,0:T(8,128)} %param.11) | copy-start | bytes 1572868
  6.5 149.7 %copy-start.2 = (f32[4,16,2048]{2,1,0:T(8,128)S(1)}, f32[4,16,2048]{2,1,0:T(8,128)}, u32[]{:S(2)}) copy-start(f32[4,16,2048]{2,1,0:T(8,128)} %param.10) | copy-start | bytes 1572868
  6.5 149.7 %copy-start.3 = (f32[4,16,2048]{2,1,0:T(8,128)S(1)}, f32[4,16,2048]{2,1,0:T(8,128)}, u32[]{:S(2)}) copy-start(f32[4,16,2048]{2,1,0:T(8,128)} %param.9) | copy-start | bytes 1572868
  6.5 149.7 %copy-start = (f32[2,4,16,2048]{3,2,1,0:T(8,128)S(1)}, f32[2,4,16,2048]{3,2,1,0:T(8,128)}, u32[]{:S(2)}) copy-start(f32[2,4,16,2048]{3,2,1,0:T(8,128)} %param.8) | copy-start | bytes 3145732
  6.5 124.4 %all-gather.2.cloned.1.call-start = ((), (), s32[]{:S(2)}) async-start(), calls=%async_computation | async-start | bytes 17301504 | tf_op jit(solution)/shard_map/all_gather | solution.py:59
  132.7 6.2 %collective-permute-start = (f32[1,4,2,2048]{3,2,1,0:T(2,128)S(1)}, f32[1,4,2,2048]{3,2,1,0:T(2,128)S(1)}, u32[]{:S(2)}, u32[]{:S(2)}) collective-permute-start(f32[1,4,2,2048]{3,2,1,0:T(2,128)S(1)} %get-tuple-element.56), channel_id=1, source_target_pairs={{1,0},{2,1},{3,2},{4,3},{5,4},{6,5},{7,6},{9,8},{10,9},{11,10},{12... | collective-permute-start | bytes 196616 | tf_op jit(solution)/shard_map/ppermute | solution.py:19
  134.6 8.3 %collective-permute-start.1 = (f32[1,4,2,2048]{3,2,1,0:T(2,128)S(1)}, f32[1,4,2,2048]{3,2,1,0:T(2,128)S(1)}, u32[]{:S(2)}, u32[]{:S(2)}) collective-permute-start(f32[1,4,2,2048]{3,2,1,0:T(2,128)S(1)} %get-tuple-element.57), channel_id=1, source_target_pairs={{0,1},{1,2},{2,3},{3,4},{4,5},{5,6},{6,7},{8,9},{9,10},{10,11},{11... | collective-permute-start | bytes 196616 | tf_op jit(solution)/shard_map/ppermute | solution.py:17
  146.0 6.2 %collective-permute-start.2 = (f32[1,4,2,2048]{3,2,1,0:T(2,128)S(1)}, f32[1,4,2,2048]{3,2,1,0:T(2,128)S(1)}, u32[]{:S(2)}, u32[]{:S(2)}) collective-permute-start(f32[1,4,2,2048]{3,2,1,0:T(2,128)S(1)} %get-tuple-element.42), channel_id=1, source_target_pairs={{1,0},{2,1},{3,2},{4,3},{5,4},{6,5},{7,6},{9,8},{10,9},{11,10},{12... | collective-permute-start | bytes 196616 | tf_op jit(solution)/shard_map/ppermute | solution.py:19
  148.0 8.3 %collective-permute-start.3 = (f32[1,4,2,2048]{3,2,1,0:T(2,128)S(1)}, f32[1,4,2,2048]{3,2,1,0:T(2,128)S(1)}, u32[]{:S(2)}, u32[]{:S(2)}) collective-permute-start(f32[1,4,2,2048]{3,2,1,0:T(2,128)S(1)} %get-tuple-element.43), channel_id=1, source_target_pairs={{0,1},{1,2},{2,3},{3,4},{4,5},{5,6},{6,7},{8,9},{9,10},{10,11},{11... | collective-permute-start | bytes 196616 | tf_op jit(solution)/shard_map/ppermute | solution.py:17
  157.8 6.2 %collective-permute-start.4 = (f32[1,4,2,2048]{3,2,1,0:T(2,128)S(1)}, f32[1,4,2,2048]{3,2,1,0:T(2,128)S(1)}, u32[]{:S(2)}, u32[]{:S(2)}) collective-permute-start(f32[1,4,2,2048]{3,2,1,0:T(2,128)S(1)} %get-tuple-element.28), channel_id=1, source_target_pairs={{1,0},{2,1},{3,2},{4,3},{5,4},{6,5},{7,6},{9,8},{10,9},{11,10},{12... | collective-permute-start | bytes 196616 | tf_op jit(solution)/shard_map/ppermute | solution.py:19
  159.7 8.3 %collective-permute-start.5 = (f32[1,4,2,2048]{3,2,1,0:T(2,128)S(1)}, f32[1,4,2,2048]{3,2,1,0:T(2,128)S(1)}, u32[]{:S(2)}, u32[]{:S(2)}) collective-permute-start(f32[1,4,2,2048]{3,2,1,0:T(2,128)S(1)} %get-tuple-element.29), channel_id=1, source_target_pairs={{0,1},{1,2},{2,3},{3,4},{4,5},{5,6},{6,7},{8,9},{9,10},{10,11},{11... | collective-permute-start | bytes 196616 | tf_op jit(solution)/shard_map/ppermute | solution.py:17
Sparse Core Ops, SparseCore 0:
  9.9 120.9 all-gather.1
where the time goes:
time: 178 us; the launch traced here: 176 us
  waiting for transfers between devices  134 us (75%)
  starting transfers between devices  17.6 us (10%)
  between operations  15.5 us (9%)
  other arithmetic  6.17 us (3%)
  local copies, waits for them, and re-layouts  3.37 us (2%)
    all_gather x1, waiting for transfers between devices, shards(): piece = lax.all_gather(ensemble, 'particle', axis=0, tiled=True)  120 us
    ppermute x3, waiting for transfers between devices, padded_2(): lax.ppermute(tail, axis, [(i, (i + 1) % count) for i in range(ends)])  12.1 us
    ppermute x3, starting transfers between devices, padded_2(): lax.ppermute(tail, axis, [(i, (i + 1) % count) for i in range(ends)])  11.8 us
    ppermute x3, starting transfers between devices, padded_2(): lax.ppermute(head, axis, [((i + 1) % count, i) for i in range(ends)])  5.76 us
    add x3, other arithmetic, step_strip(): field - cross * dx - along * dy + 0.1 * lap + 0.1 * vmix  5.08 us
  transfers between devices with their start and end apart: 7, of which 7 were waited for; matrix products, arithmetic and copies ran while one was open for 1% of the time, Pallas kernels for 0%

commit v1 on v0

v1 whole, which is shorter than its diff:
```python
import functools

import jax
import jax.numpy as jnp
from jax import lax
from jax.experimental import pallas as pl
from jax.experimental.pallas import tpu as pltpu
from jax.sharding import PartitionSpec as P

ITERS = 3
MESH = pl.DeviceIdType.MESH
EDGE = 128
TOP = 8
BLOCKS = 2
SPAN = 512


def kernel(
    anc, ens, vel, obs, gain, forc, out,
    inboxes, outbox, u0, u1, u2, vx, vy, keep, add, raw_o, raw_f, head_s, tail_s, head_r, tail_r,
    load_sem, own_sem, s1, r1, s2, r2, hs_sem, hr_sem,
):
    n = lax.axis_size("particle")
    tiles = lax.axis_size("tile")
    me = lax.axis_index("particle")
    t = lax.axis_index("tile")
    levels, rows, cols = obs.shape
    halves = rows // 8
    width = cols // BLOCKS
    cw = width * levels * halves // n
    per_row = width // cw
    fields = (u0, u1, u2)
    has_up, has_down = t > 0, t < tiles - 1

    loads = [
        pltpu.make_async_copy(vel.at[0], vx, load_sem.at[0]),
        pltpu.make_async_copy(vel.at[1], vy, load_sem.at[1]),
        pltpu.make_async_copy(gain, keep, load_sem.at[2]),
        pltpu.make_async_copy(obs, raw_o, load_sem.at[3]),
        pltpu.make_async_copy(forc.at[0], raw_f, load_sem.at[4]),
    ]
    for load in loads:
        load.start()

    def place(j, b, top, left):
        level = j // (halves * per_row)
        half = (j // per_row) % halves
        return (
            level,
            pl.ds(pl.multiple_of(top + half * 8, 8), 8),
            pl.ds(pl.multiple_of(left + b * width + (j % per_row) * cw, 128), cw),
        )

    def partner(r):
        return (me + (r % 4) * (n // 4) + r // 4) % n

    barrier = pltpu.get_barrier_semaphore()

    def greet(r, carry):
        pl.semaphore_signal(barrier, inc=1, device_id={"particle": partner(r)}, device_id_type=MESH)
        return carry

    lax.fori_loop(1, n, greet, 0)

    @pl.when(has_up)
    def _():
        pl.semaphore_signal(barrier, inc=1, device_id={"tile": t - 1}, device_id_type=MESH)

    @pl.when(has_down)
    def _():
        pl.semaphore_signal(barrier, inc=1, device_id={"tile": t + 1}, device_id_type=MESH)

    pl.semaphore_wait(barrier, n - 1 + jnp.where(has_up, 1, 0) + jnp.where(has_down, 1, 0))

    own1 = []
    for b in range(BLOCKS):

        def spread(r, carry, b=b):
            j = partner(r)
            pltpu.make_async_remote_copy(
                src_ref=ens.at[(0,) + place(j, b, 0, 0)],
                dst_ref=inboxes[b].at[me],
                send_sem=s1.at[b],
                recv_sem=r1.at[b],
                device_id={"particle": j},
                device_id_type=MESH,
            ).start()
            return carry

        lax.fori_loop(1, n, spread, 0)
        copy = pltpu.make_async_copy(ens.at[(0,) + place(me, b, 0, 0)], inboxes[b].at[me], own_sem.at[b])
        copy.start()
        own1.append(copy)

    for load in loads:
        load.wait()

    def prepare(i, carry):
        c = pl.ds(pl.multiple_of(i * SPAN, 128), SPAN)
        for l in range(levels):
            g = keep[l, :, c]
            add[l, :, c] = g * raw_o[l, :, c] + raw_f[l, :, c]
            keep[l, :, c] = 0.4 - g
            vx[l, :, c] = vx[l, :, c] * (1.0 / 12.0)
            vy[l, :, c] = vy[l, :, c] * (1.0 / 12.0)
        return carry

    lax.fori_loop(0, cols // SPAN, prepare, 0)

    own2 = []
    for b in range(BLOCKS):
        whole = inboxes[b].at[pl.ds(0, n - 1)]
        pltpu.make_async_copy(whole, whole, r1.at[b]).wait()
        own1[b].wait()

        def choose(p, carry, b=b):
            outbox[b, p] = inboxes[b][anc[p]]
            return carry

        lax.fori_loop(0, n, choose, 0)

        def deliver(r, carry, b=b):
            p = partner(r)
            pltpu.make_async_remote_copy(
                src_ref=outbox.at[b, p],
                dst_ref=u0.at[place(me, b, TOP, EDGE)],
                send_sem=s2.at[b],
                recv_sem=r2.at[b],
                device_id={"particle": p},
                device_id_type=MESH,
            ).start()
            return carry

        lax.fori_loop(1, n, deliver, 0)
        copy = pltpu.make_async_copy(outbox.at[b, me], u0.at[place(me, b, TOP, EDGE)], own_sem.at[BLOCKS + b])
        copy.start()
        own2.append(copy)

    for b in range(BLOCKS):
        whole = inboxes[b].at[pl.ds(0, n - 1)]
        pltpu.make_async_copy(whole, whole, r2.at[b]).wait()
        own2[b].wait()

    centre = pl.ds(EDGE, cols)
    for step in range(ITERS):
        u = fields[step]

        up = pltpu.make_async_remote_copy(
            src_ref=head_s.at[step], dst_ref=tail_r.at[step],
            send_sem=hs_sem.at[2 * step], recv_sem=hr_sem.at[2 * step],
            device_id={"tile": t - 1}, device_id_type=MESH,
        )
        down = pltpu.make_async_remote_copy(
            src_ref=tail_s.at[step], dst_ref=head_r.at[step],
            send_sem=hs_sem.at[2 * step + 1], recv_sem=hr_sem.at[2 * step + 1],
            device_id={"tile": t + 1}, device_id_type=MESH,
        )
        for l in range(levels):
            head_s[step, 2 * l : 2 * l + 2, :] = u[l, TOP : TOP + 2, centre]
        pl.when(has_up)(up.start)
        for l in range(levels):
            tail_s[step, 2 * l : 2 * l + 2, :] = u[l, TOP + rows - 2 : TOP + rows, centre]
        pl.when(has_down)(down.start)

        for l in range(levels):
            u[l, TOP : TOP + rows, 0:EDGE] = u[l, TOP : TOP + rows, cols : cols + EDGE]
            u[l, TOP : TOP + rows, EDGE + cols :] = u[l, TOP : TOP + rows, EDGE : 2 * EDGE]

        @pl.when(has_up)
        def _(u=u, step=step, down=down):
            down.wait_recv()
            for l in range(levels):
                u[l, TOP - 2 : TOP, centre] = head_r[step, 2 * l : 2 * l + 2, :]

        @pl.when(jnp.logical_not(has_up))
        def _(u=u):
            for l in range(levels):
                u[l, TOP - 2 : TOP, centre] = jnp.zeros((2, cols), jnp.float32)

        @pl.when(has_down)
        def _(u=u, step=step, up=up):
            up.wait_recv()
            for l in range(levels):
                u[l, TOP + rows : TOP + rows + 2, centre] = tail_r[step, 2 * l : 2 * l + 2, :]

        @pl.when(jnp.logical_not(has_down))
        def _(u=u):
            for l in range(levels):
                u[l, TOP + rows : TOP + rows + 2, centre] = jnp.zeros((2, cols), jnp.float32)

        def advance(i, carry, u=u, step=step):
            c = pl.multiple_of(i * SPAN, 128)
            mid = pl.ds(pl.multiple_of(c + EDGE, 128), SPAN)
            own = pl.ds(c, SPAN)
            wide = SPAN + 2 * EDGE
            for half in range(halves):
                top = TOP + 8 * half
                here = [u[l, top : top + 8, mid] for l in range(levels)]
                for l in range(levels):
                    around = u[l, top : top + 8, pl.ds(c, wide)]
                    east = pltpu.roll(around, wide - 1, 1)[:, EDGE : EDGE + SPAN]
                    west = pltpu.roll(around, 1, 1)[:, EDGE : EDGE + SPAN]
                    east2 = pltpu.roll(around, wide - 2, 1)[:, EDGE : EDGE + SPAN]
                    west2 = pltpu.roll(around, 2, 1)[:, EDGE : EDGE + SPAN]
                    south = u[l, top + 1 : top + 9, mid]
                    north = u[l, top - 1 : top + 7, mid]
                    south2 = u[l, top + 2 : top + 10, mid]
                    north2 = u[l, top - 2 : top + 6, mid]
                    r = pl.ds(8 * half, 8)
                    mixed = (east + west) + (south + north) + (here[min(l + 1, levels - 1)] + here[max(l - 1, 0)])
                    value = (
                        keep[l, r, own] * here[l]
                        + add[l, r, own]
                        + 0.1 * mixed
                        + vx[l, r, own] * ((east2 - west2) - 8.0 * (east - west))
                        + vy[l, r, own] * ((south2 - north2) - 8.0 * (south - north))
                    )
                    if step == ITERS - 1:
                        out[0, l, r, own] = value
                    else:
                        fields[step + 1][l, top : top + 8, mid] = value
            return carry

        lax.fori_loop(0, cols // SPAN, advance, 0)

        pl.when(has_up)(up.wait_send)
        pl.when(has_down)(down.wait_send)

    for b in range(BLOCKS):
        whole = inboxes[b].at[pl.ds(0, n - 1)]
        pltpu.make_async_copy(whole, whole, s1.at[b]).wait()
        pltpu.make_async_copy(whole, whole, s2.at[b]).wait()


def shards(ensemble, ancestor, velocity, observed, nudge_gain, forcing):
    _, levels, rows, cols = ensemble.shape
    n = lax.axis_size("particle")
    chunk = cols // BLOCKS * levels * (rows // 8) // n
    strip = (levels, rows, cols)
    padded = (levels, rows + 2 * TOP, cols + 2 * EDGE)
    vmem = functools.partial(pltpu.VMEM, dtype=jnp.float32)
    anywhere = pl.BlockSpec(memory_space=pl.ANY)
    return pl.pallas_call(
        kernel,
        out_shape=jax.ShapeDtypeStruct(ensemble.shape, jnp.float32),
        in_specs=[pl.BlockSpec(memory_space=pltpu.SMEM)] + [anywhere] * 5,
        out_specs=pl.BlockSpec(memory_space=pltpu.VMEM),
        scratch_shapes=[
            [vmem((n, 8, chunk))] * BLOCKS, vmem((BLOCKS, n, 8, chunk)),
            vmem(padded), vmem(padded), vmem(padded),
            vmem(strip), vmem(strip), vmem(strip), vmem(strip), vmem(strip), vmem(strip),
            vmem((ITERS, 2 * levels, cols)), vmem((ITERS, 2 * levels, cols)),
            vmem((ITERS, 2 * levels, cols)), vmem((ITERS, 2 * levels, cols)),
            pltpu.SemaphoreType.DMA((5,)),
            pltpu.SemaphoreType.DMA((2 * BLOCKS,)),
            pltpu.SemaphoreType.DMA((BLOCKS,)),
            pltpu.SemaphoreType.DMA((BLOCKS,)),
            pltpu.SemaphoreType.DMA((BLOCKS,)),
            pltpu.SemaphoreType.DMA((BLOCKS,)),
            pltpu.SemaphoreType.DMA((2 * ITERS,)),
            pltpu.SemaphoreType.DMA((2 * ITERS,)),
        ],
        compiler_params=pltpu.CompilerParams(
            collective_id=0, has_side_effects=True, vmem_limit_bytes=32 << 20
        ),
    )(ancestor, ensemble, velocity, observed, nudge_gain, forcing)


def solution(mesh):
    placed = (
        P("particle", None, "tile", None),
        P(),
        P(None, None, "tile", None),
        P(None, "tile", None),
        P(None, "tile", None),
        P("particle", None, "tile", None),
    )
    return jax.shard_map(
        shards,
        mesh=mesh,
        in_specs=placed,
        out_specs=P("particle", None, "tile", None),
        check_vma=False,
    )
```

time: 178 us -> 60.6 us (0.34)
  waiting for transfers between devices: 134 us -> 0 us
  Pallas kernels: 0 us -> 53.4 us
  starting transfers between devices: 17.6 us -> 0 us
  between operations: 15.5 us -> 0.02 us
  other arithmetic: 6.17 us -> 0 us
  local copies, waits for them, and re-layouts: 3.37 us -> 6.84 us
    all_gather x1 -> x0, waiting for transfers between devices: 120 us -> none  [shards(): piece = lax.all_gather(ensemble, 'particle', axis=0, tiled=True)]
    pallas_call x0 -> x1, Pallas kernels: none -> 53.4 us  [shards(): pl.pallas_call(kernel, out_shape=jax.ShapeDtypeStruct(ensemble.shape, jnp...]
    ppermute x6 -> x0, starting transfers between devices: 17.5 us -> none  [the longest x3 11.8 us: padded_2(): lax.ppermute(tail, axis, [(i, (i + 1) % count) for i in range(ends)])]
    ppermute x6 -> x0, waiting for transfers between devices: 12.8 us -> none  [the longest x3 12.1 us: padded_2(): lax.ppermute(tail, axis, [(i, (i + 1) % count) for i in range(ends)])]
    unnamed x8 -> x13, local copies, waits for them, and re-layouts: 0.01 us -> 6.84 us
    add x3 -> x0, other arithmetic: 5.08 us -> none  [step_strip(): field - cross * dx - along * dy + 0.1 * lap + 0.1 * vmix]
    slice x21 -> x0, local copies, waits for them, and re-layouts: 2.07 us -> none  [the longest x6 0.85 us: step_strip(): east = jnp.roll(field, -1, 3)]
  transfers between devices with their start and end apart: 7 -> 0, of which waited for: 7 -> 0; matrix products, arithmetic and copies ran while one was open for 1% -> 0% of each run, Pallas kernels for 0% -> 0%
where the time goes in v1:
time: 60.6 us; the launch traced here: 60.3 us
  Pallas kernels  53.4 us (88%)
  local copies, waits for them, and re-layouts  6.84 us (11%)
    pallas_call x1, Pallas kernels, shards(): pl.pallas_call(kernel, out_shape=jax.ShapeDtypeStruct(ensemble.shape, jnp...  53.4 us
    unnamed x13, local copies, waits for them, and re-layouts  6.84 us

profile of v1, /device:TPU:32, one launch (start us, length us, event | category | flops | bytes accessed | tf_op | source)
XLA Modules:
  0.0 60.3 jit_solution(155448421135808695)
XLA Ops:
  0.0 0.0 copy-start
  0.0 1.2 %copy-done = f32[2,4,16,2048]{3,2,1,0:T(8,128)S(1)} copy-done((f32[2,4,16,2048]{3,2,1,0:T(8,128)S(1)}, f32[2,4,16,2048]{3,2,1,0:T(8,128)}, u32[]{:S(2)}) %copy-start) | copy-done | bytes 1048600
  1.2 0.0 copy-start.1
  1.2 1.0 %copy-done.1 = f32[1,4,16,2048]{3,2,1,0:T(8,128)S(1)} copy-done((f32[1,4,16,2048]{3,2,1,0:T(8,128)S(1)}, f32[1,4,16,2048]{3,2,1,0:T(8,128)}, u32[]{:S(2)}) %copy-start.1) | copy-done | bytes 524312
  2.3 0.0 copy-start.2
  2.3 1.0 %copy-done.2 = f32[4,16,2048]{2,1,0:T(8,128)S(1)} copy-done((f32[4,16,2048]{2,1,0:T(8,128)S(1)}, f32[4,16,2048]{2,1,0:T(8,128)}, u32[]{:S(2)}) %copy-start.2) | copy-done | bytes 524312
  3.3 0.0 copy-start.3
  3.3 1.0 %copy-done.3 = f32[4,16,2048]{2,1,0:T(8,128)S(1)} copy-done((f32[4,16,2048]{2,1,0:T(8,128)S(1)}, f32[4,16,2048]{2,1,0:T(8,128)}, u32[]{:S(2)}) %copy-start.3) | copy-done | bytes 524312
  4.4 0.0 copy-start.4
  4.4 1.0 %copy-done.4 = f32[1,4,16,2048]{3,2,1,0:T(8,128)S(1)} copy-done((f32[1,4,16,2048]{3,2,1,0:T(8,128)S(1)}, f32[1,4,16,2048]{3,2,1,0:T(8,128)}, u32[]{:S(2)}) %copy-start.4) | copy-done | bytes 524312
  5.4 0.0 copy-start.5
  5.4 0.7 %copy-done.5 = s32[32]{0:T(128)S(1)} copy-done((s32[32]{0:T(128)S(1)}, s32[32]{0:T(128)}, u32[]{:S(2)}) %copy-start.5) | copy-done | bytes 152
  6.0 53.4 %shard_map.64 = f32[1,4,16,2048]{3,2,1,0:T(8,128)S(1)} custom-call(s32[32]{0:T(128)S(1)} %copy-done.5, f32[1,4,16,2048]{3,2,1,0:T(8,128)S(1)} %copy-done.1, f32[2,4,16,2048]{3,2,1,0:T(8,128)S(1)} %copy-done, f32[4,16,2048]{2,1,0:T(8,128)S(1)} %copy-done.2, f32[4,16,2048]{2,1,0:T(8,128)S(1)} %copy-done.3, f32[1,4,16,2048]{3,2,1,0:T(8,128)S(1)} %copy-done.4), custom_call_target="tpu_custom_call" | custom-call | tf_op jit(solution)/shard_map/pallas_call | solution.py:243
  59.5 0.8 %copy.8 = f32[1,4,16,2048]{3,2,1,0:T(8,128)} copy(f32[1,4,16,2048]{3,2,1,0:T(8,128)S(1)} %shard_map.64) | data formatting | bytes 1048576
Async XLA Ops:
  0.0 1.2 %copy-start = (f32[2,4,16,2048]{3,2,1,0:T(8,128)S(1)}, f32[2,4,16,2048]{3,2,1,0:T(8,128)}, u32[]{:S(2)}) copy-start(f32[2,4,16,2048]{3,2,1,0:T(8,128)} %vel.1) | copy-start | bytes 3145732
  1.2 1.0 %copy-start.1 = (f32[1,4,16,2048]{3,2,1,0:T(8,128)S(1)}, f32[1,4,16,2048]{3,2,1,0:T(8,128)}, u32[]{:S(2)}) copy-start(f32[1,4,16,2048]{3,2,1,0:T(8,128)} %ens.1) | copy-start | bytes 1572868
  2.3 1.0 %copy-start.2 = (f32[4,16,2048]{2,1,0:T(8,128)S(1)}, f32[4,16,2048]{2,1,0:T(8,128)}, u32[]{:S(2)}) copy-start(f32[4,16,2048]{2,1,0:T(8,128)} %obs.1) | copy-start | bytes 1572868
  3.3 1.0 %copy-start.3 = (f32[4,16,2048]{2,1,0:T(8,128)S(1)}, f32[4,16,2048]{2,1,0:T(8,128)}, u32[]{:S(2)}) copy-start(f32[4,16,2048]{2,1,0:T(8,128)} %gain.1) | copy-start | bytes 1572868
  4.4 1.0 %copy-start.4 = (f32[1,4,16,2048]{3,2,1,0:T(8,128)S(1)}, f32[1,4,16,2048]{3,2,1,0:T(8,128)}, u32[]{:S(2)}) copy-start(f32[1,4,16,2048]{3,2,1,0:T(8,128)} %forc.1) | copy-start | bytes 1572868
  5.4 0.7 %copy-start.5 = (s32[32]{0:T(128)S(1)}, s32[32]{0:T(128)}, u32[]{:S(2)}) copy-start(s32[32]{0:T(128)} %anc.1) | copy-start | bytes 388

commit v2 on v0

v2 whole, which is shorter than its diff:
```python
import functools

import jax
import jax.numpy as jnp
from jax import lax
from jax.experimental import pallas as pl
from jax.experimental.pallas import tpu as pltpu
from jax.sharding import PartitionSpec as P

ITERS = 3
MESH = pl.DeviceIdType.MESH
LANES = 128
GROUP = 4
TILE = 8


def kernel(
    anc, ens, vel, obs, gain, forc, out,
    raw, state, inboxes, outbox, fields, last, vx, vy, keep, add,
    load_sem, s1, r1, s2, r2, hs, hr,
):
    n = lax.axis_size("particle")
    tiles = lax.axis_size("tile")
    me = lax.axis_index("particle")
    t = lax.axis_index("tile")
    levels, rows, cols = obs.shape
    pairs = rows * levels // TILE
    blocks = pairs // 2
    per_pair = n // 2
    strips = cols // LANES
    has_up, has_down = t > 0, t < tiles - 1

    sources = [ens.at[0], vel.at[0], vel.at[1], gain, obs, forc.at[0]]
    loads = [pltpu.make_async_copy(s, raw.at[i], load_sem.at[i]) for i, s in enumerate(sources)]
    for load in loads:
        load.start()

    def partner(r):
        return (me + (r % 4) * (n // 4) + r // 4) % n

    barrier = pltpu.get_barrier_semaphore()

    def greet(r, carry):
        pl.semaphore_signal(barrier, inc=1, device_id={"particle": partner(r)}, device_id_type=MESH)
        return carry

    lax.fori_loop(1, n, greet, 0)

    @pl.when(has_up)
    def _():
        pl.semaphore_signal(barrier, inc=1, device_id={"tile": t - 1}, device_id_type=MESH)

    @pl.when(has_down)
    def _():
        pl.semaphore_signal(barrier, inc=1, device_id={"tile": t + 1}, device_id_type=MESH)

    loads[0].wait()
    for k in range(strips):
        for l in range(levels):
            state[k, pl.ds(l, rows, stride=levels), :] = raw[0, l, :, LANES * k : LANES * (k + 1)]

    def piece(j, b, top):
        pair = b + (j // per_pair) * (pairs - 1 - 2 * b)
        return (j % per_pair, pl.ds(pl.multiple_of(top + pair * TILE, TILE), TILE))

    def scatter(b):
        def send(r, carry):
            j = partner(r)
            pltpu.make_async_remote_copy(
                src_ref=state.at[piece(j, b, 0)],
                dst_ref=inboxes[b].at[me],
                send_sem=s1.at[b],
                recv_sem=r1.at[b],
                device_id={"particle": j},
                device_id_type=MESH,
            ).start()
            return carry

        lax.fori_loop(1, n, send, 0)
        inboxes[b][me] = state[piece(me, b, 0)]

    def all_of(b, sem):
        whole = inboxes[b].at[pl.ds(0, n - 1)]
        pltpu.make_async_copy(whole, whole, sem.at[b]).wait()

    def deliver(b):
        all_of(b, r1)
        for p in range(n):
            outbox[b, p] = inboxes[b][anc[p]]

        def send(r, carry):
            p = partner(r)
            pltpu.make_async_remote_copy(
                src_ref=outbox.at[b, p],
                dst_ref=fields[0].at[piece(me, b, TILE)],
                send_sem=s2.at[b],
                recv_sem=r2.at[b],
                device_id={"particle": p},
                device_id_type=MESH,
            ).start()
            return carry

        lax.fori_loop(1, n, send, 0)
        fields[0][piece(me, b, TILE)] = outbox[b, me]

    def halos(step):
        u = fields[step]
        up = pltpu.make_async_remote_copy(
            src_ref=u.at[:, pl.ds(TILE, TILE)],
            dst_ref=u.at[:, pl.ds(TILE * (pairs + 1), TILE)],
            send_sem=hs.at[2 * step], recv_sem=hr.at[2 * step],
            device_id={"tile": t - 1}, device_id_type=MESH,
        )
        down = pltpu.make_async_remote_copy(
            src_ref=u.at[:, pl.ds(TILE * pairs, TILE)],
            dst_ref=u.at[:, pl.ds(0, TILE)],
            send_sem=hs.at[2 * step + 1], recv_sem=hr.at[2 * step + 1],
            device_id={"tile": t + 1}, device_id_type=MESH,
        )
        return up, down

    def send_halos(step):
        up, down = halos(step)
        pl.when(has_up)(up.start)
        pl.when(has_down)(down.start)

    def wait_halos(step):
        up, down = halos(step)
        pl.when(has_up)(down.wait_recv)
        pl.when(has_down)(up.wait_recv)

    def advance(step, some):
        u = fields[step]

        def group(i, carry):
            level = lax.broadcasted_iota(jnp.int32, (TILE, LANES), 0) % levels
            lane = lax.broadcasted_iota(jnp.int32, (TILE, LANES), 1)
            first = i * GROUP
            ks = [(first + strips - 1) % strips] + [first + k for k in range(GROUP)] + [(first + GROUP) % strips]
            for pair in some:
                top = TILE * (pair + 1)
                r = pl.ds(TILE * pair, TILE)
                row = [u[k, top : top + TILE, :] for k in ks]
                left = [pltpu.roll(x, LANES - 1, 1) for x in row[1:]]
                left2 = [pltpu.roll(x, LANES - 2, 1) for x in row[1:]]
                right = [pltpu.roll(x, 1, 1) for x in row[:-1]]
                right2 = [pltpu.roll(x, 2, 1) for x in row[:-1]]
                for g in range(GROUP):
                    k = first + g
                    here = row[g + 1]
                    east = jnp.where(lane < LANES - 1, left[g], left[g + 1])
                    east2 = jnp.where(lane < LANES - 2, left2[g], left2[g + 1])
                    west = jnp.where(lane < 1, right[g], right[g + 1])
                    west2 = jnp.where(lane < 2, right2[g], right2[g + 1])
                    south = u[k, top + levels : top + TILE + levels, :]
                    north = u[k, top - levels : top + TILE - levels, :]
                    south2 = u[k, top + TILE : top + 2 * TILE, :]
                    north2 = u[k, top - TILE : top, :]
                    upper = jnp.where(level == levels - 1, here, pltpu.roll(here, TILE - 1, 0))
                    lower = jnp.where(level == 0, here, pltpu.roll(here, 1, 0))
                    mixed = (east + west) + (south + north) + (upper + lower)
                    value = (
                        keep[k, r, :] * here
                        + add[k, r, :]
                        + 0.1 * mixed
                        + vx[k, r, :] * ((east2 - west2) - 8.0 * (east - west))
                        + vy[k, r, :] * ((south2 - north2) - 8.0 * (south - north))
                    )
                    if step == ITERS - 1:
                        last[k, r, :] = value
                    else:
                        fields[step + 1][k, top : top + TILE, :] = value
            return carry

        lax.fori_loop(0, strips // GROUP, group, 0)

    pl.semaphore_wait(barrier, n - 1 + jnp.where(has_up, 1, 0) + jnp.where(has_down, 1, 0))

    scatter(0)
    scatter(1)

    for u in fields:

        @pl.when(jnp.logical_not(has_up))
        def _(u=u):
            u[:, 0:TILE, :] = jnp.zeros((strips, TILE, LANES), jnp.float32)

        @pl.when(jnp.logical_not(has_down))
        def _(u=u):
            u[:, TILE * (pairs + 1) :, :] = jnp.zeros((strips, TILE, LANES), jnp.float32)

    for load in loads[1:]:
        load.wait()

    for k in range(strips):
        c = slice(LANES * k, LANES * (k + 1))
        for l in range(levels):
            r = pl.ds(l, rows, stride=levels)
            vx[k, r, :] = raw[1, l, :, c] * (1.0 / 12.0)
            vy[k, r, :] = raw[2, l, :, c] * (1.0 / 12.0)
            keep[k, r, :] = 0.4 - raw[3, l, :, c]
            add[k, r, :] = raw[3, l, :, c] * raw[4, l, :, c] + raw[5, l, :, c]

    deliver(0)
    scatter(2)
    deliver(1)
    scatter(3)
    all_of(0, r2)
    send_halos(0)
    deliver(2)
    all_of(1, r2)
    wait_halos(0)
    advance(0, (0, pairs - 1))
    send_halos(1)
    deliver(3)
    all_of(2, r2)
    advance(0, (1, pairs - 2))
    wait_halos(1)
    advance(1, (0, pairs - 1))
    send_halos(2)
    all_of(3, r2)
    advance(0, range(2, pairs - 2))
    advance(1, range(1, pairs - 1))
    wait_halos(2)
    advance(2, range(pairs))
    for k in range(strips):
        for l in range(levels):
            out[0, l, :, LANES * k : LANES * (k + 1)] = last[k, pl.ds(l, rows, stride=levels), :]

    for step in range(ITERS):
        up, down = halos(step)
        pl.when(has_up)(up.wait_send)
        pl.when(has_down)(down.wait_send)
    for b in range(blocks):
        all_of(b, s1)
        all_of(b, s2)


def shards(ensemble, ancestor, velocity, observed, nudge_gain, forcing):
    _, levels, rows, cols = ensemble.shape
    n = lax.axis_size("particle")
    blocks = rows * levels // TILE // 2
    strip = (cols // LANES, rows * levels, LANES)
    padded = (cols // LANES, rows * levels + 2 * TILE, LANES)
    vmem = functools.partial(pltpu.VMEM, dtype=jnp.float32)
    anywhere = pl.BlockSpec(memory_space=pl.ANY)
    dma = pltpu.SemaphoreType.DMA
    return pl.pallas_call(
        kernel,
        out_shape=jax.ShapeDtypeStruct(ensemble.shape, jnp.float32),
        in_specs=[pl.BlockSpec(memory_space=pltpu.SMEM)] + [anywhere] * 5,
        out_specs=pl.BlockSpec(memory_space=pltpu.VMEM),
        scratch_shapes=[
            vmem((6, levels, rows, cols)),
            vmem(strip),
            [vmem((n, TILE, LANES))] * blocks,
            vmem((blocks, n, TILE, LANES)),
            [vmem(padded)] * ITERS,
            vmem(strip),
            vmem(strip), vmem(strip), vmem(strip), vmem(strip),
            dma((6,)), dma((blocks,)), dma((blocks,)), dma((blocks,)), dma((blocks,)),
            dma((2 * ITERS,)), dma((2 * ITERS,)),
        ],
        compiler_params=pltpu.CompilerParams(
            collective_id=0, has_side_effects=True, vmem_limit_bytes=60 << 20
        ),
    )(ancestor, ensemble, velocity, observed, nudge_gain, forcing)


def solution(mesh):
    placed = (
        P("particle", None, "tile", None),
        P(),
        P(None, None, "tile", None),
        P(None, "tile", None),
        P(None, "tile", None),
        P("particle", None, "tile", None),
    )
    return jax.shard_map(
        shards,
        mesh=mesh,
        in_specs=placed,
        out_specs=P("particle", None, "tile", None),
        check_vma=False,
    )
```

time: 178 us -> 49.1 us (0.28)
  waiting for transfers between devices: 134 us -> 0 us
  Pallas kernels: 0 us -> 46.8 us
  starting transfers between devices: 17.6 us -> 0 us
  between operations: 15.5 us -> 0.01 us
  other arithmetic: 6.17 us -> 0 us
    all_gather x1 -> x0, waiting for transfers between devices: 120 us -> none  [shards(): piece = lax.all_gather(ensemble, 'particle', axis=0, tiled=True)]
    pallas_call x0 -> x1, Pallas kernels: none -> 46.8 us  [shards(): pl.pallas_call(kernel, out_shape=jax.ShapeDtypeStruct(ensemble.shape, jnp...]
    ppermute x6 -> x0, starting transfers between devices: 17.5 us -> none  [the longest x3 11.8 us: padded_2(): lax.ppermute(tail, axis, [(i, (i + 1) % count) for i in range(ends)])]
    ppermute x6 -> x0, waiting for transfers between devices: 12.8 us -> none  [the longest x3 12.1 us: padded_2(): lax.ppermute(tail, axis, [(i, (i + 1) % count) for i in range(ends)])]
    add x3 -> x0, other arithmetic: 5.08 us -> none  [step_strip(): field - cross * dx - along * dy + 0.1 * lap + 0.1 * vmix]
    slice x21 -> x0, local copies, waits for them, and re-layouts: 2.07 us -> none  [the longest x6 0.85 us: step_strip(): east = jnp.roll(field, -1, 3)]
    unnamed x8 -> x1, local copies, waits for them, and re-layouts: 0.01 us -> 1.87 us
  transfers between devices with their start and end apart: 7 -> 0, of which waited for: 7 -> 0; matrix products, arithmetic and copies ran while one was open for 1% -> 0% of each run, Pallas kernels for 0% -> 0%
where the time goes in v2:
time: 49.1 us; the launch traced here: 48.7 us
  Pallas kernels  46.8 us (95%)
  local copies, waits for them, and re-layouts  1.87 us (4%)
    pallas_call x1, Pallas kernels, shards(): pl.pallas_call(kernel, out_shape=jax.ShapeDtypeStruct(ensemble.shape, jnp...  46.8 us
    unnamed x1, local copies, waits for them, and re-layouts  1.87 us

profile of v2, /device:TPU:32, one launch (start us, length us, event | category | flops | bytes accessed | tf_op | source)
XLA Modules:
  0.0 48.7 jit_solution(7293357816192695779)
XLA Ops:
  0.0 46.8 %shard_map.64 = f32[1,4,16,2048]{3,2,1,0:T(8,128)} custom-call(s32[32]{0:T(128)} %anc.1, f32[1,4,16,2048]{3,2,1,0:T(8,128)} %ens.1, f32[2,4,16,2048]{3,2,1,0:T(8,128)} %vel.1, f32[4,16,2048]{2,1,0:T(8,128)} %obs.1, f32[4,16,2048]{2,1,0:T(8,128)} %gain.1, f32[1,4,16,2048]{3,2,1,0:T(8,128)} %forc.1), custom_call_target="tpu_custom_call" | custom-call | tf_op jit(solution)/shard_map/pallas_call | solution.py:248
  46.8 1.9 %copy.8 = f32[1,4,16,2048]{3,2,1,0:T(8,128)} copy(f32[1,4,16,2048]{3,2,1,0:T(8,128)} %shard_map.64) | data formatting | bytes 1048576

commit v3 on v2

--- a/solution.py
+++ b/solution.py
@@ -11,6 +11,7 @@
 MESH = pl.DeviceIdType.MESH
 LANES = 128
 GROUP = 4
+PARTS = 2
 TILE = 8
 
 
@@ -103,33 +104,35 @@
         lax.fori_loop(1, n, send, 0)
         fields[0][piece(me, b, TILE)] = outbox[b, me]
 
-    def halos(step):
+    def halos(step, part):
         u = fields[step]
+        sem = 2 * (PARTS * step + part)
+        c = pl.ds(part * (strips // PARTS), strips // PARTS)
         up = pltpu.make_async_remote_copy(
-            src_ref=u.at[:, pl.ds(TILE, TILE)],
-            dst_ref=u.at[:, pl.ds(TILE * (pairs + 1), TILE)],
-            send_sem=hs.at[2 * step], recv_sem=hr.at[2 * step],
+            src_ref=u.at[c, pl.ds(TILE, TILE)],
+            dst_ref=u.at[c, pl.ds(TILE * (pairs + 1), TILE)],
+            send_sem=hs.at[sem], recv_sem=hr.at[sem],
             device_id={"tile": t - 1}, device_id_type=MESH,
         )
         down = pltpu.make_async_remote_copy(
-            src_ref=u.at[:, pl.ds(TILE * pairs, TILE)],
-            dst_ref=u.at[:, pl.ds(0, TILE)],
-            send_sem=hs.at[2 * step + 1], recv_sem=hr.at[2 * step + 1],
+            src_ref=u.at[c, pl.ds(TILE * pairs, TILE)],
+            dst_ref=u.at[c, pl.ds(0, TILE)],
+            send_sem=hs.at[sem + 1], recv_sem=hr.at[sem + 1],
             device_id={"tile": t + 1}, device_id_type=MESH,
         )
         return up, down
 
-    def send_halos(step):
-        up, down = halos(step)
+    def send_halos(step, part):
+        up, down = halos(step, part)
         pl.when(has_up)(up.start)
         pl.when(has_down)(down.start)
 
-    def wait_halos(step):
-        up, down = halos(step)
+    def wait_halos(step, part):
+        up, down = halos(step, part)
         pl.when(has_up)(down.wait_recv)
         pl.when(has_down)(up.wait_recv)
 
-    def advance(step, some):
+    def advance(step, some, part=0, parts=1):
         u = fields[step]
 
         def group(i, carry):
@@ -172,12 +175,14 @@
                         fields[step + 1][k, top : top + TILE, :] = value
             return carry
 
-        lax.fori_loop(0, strips // GROUP, group, 0)
+        groups = strips // GROUP // parts
+        lax.fori_loop(part * groups, (part + 1) * groups, group, 0)
 
     pl.semaphore_wait(barrier, n - 1 + jnp.where(has_up, 1, 0) + jnp.where(has_down, 1, 0))
 
     scatter(0)
     scatter(1)
+    scatter(2)
 
     for u in fields:
 
@@ -201,36 +206,42 @@
             keep[k, r, :] = 0.4 - raw[3, l, :, c]
             add[k, r, :] = raw[3, l, :, c] * raw[4, l, :, c] + raw[5, l, :, c]
 
+    edges = (0, pairs - 1)
     deliver(0)
-    scatter(2)
+    scatter(3)
     deliver(1)
-    scatter(3)
+    deliver(2)
     all_of(0, r2)
-    send_halos(0)
-    deliver(2)
+    for part in range(PARTS):
+        send_halos(0, part)
+    deliver(3)
     all_of(1, r2)
-    wait_halos(0)
-    advance(0, (0, pairs - 1))
-    send_halos(1)
-    deliver(3)
+    for part in range(PARTS):
+        wait_halos(0, part)
+        advance(0, edges, part, PARTS)
+        send_halos(1, part)
     all_of(2, r2)
     advance(0, (1, pairs - 2))
-    wait_halos(1)
-    advance(1, (0, pairs - 1))
-    send_halos(2)
+    for part in range(PARTS):
+        wait_halos(1, part)
+        advance(1, edges, part, PARTS)
+        send_halos(2, part)
     all_of(3, r2)
     advance(0, range(2, pairs - 2))
     advance(1, range(1, pairs - 1))
-    wait_halos(2)
-    advance(2, range(pairs))
+    advance(2, range(1, pairs - 1))
+    for part in range(PARTS):
+        wait_halos(2, part)
+        advance(2, edges, part, PARTS)
     for k in range(strips):
         for l in range(levels):
             out[0, l, :, LANES * k : LANES * (k + 1)] = last[k, pl.ds(l, rows, stride=levels), :]
 
     for step in range(ITERS):
-        up, down = halos(step)
-        pl.when(has_up)(up.wait_send)
-        pl.when(has_down)(down.wait_send)
+        for part in range(PARTS):
+            up, down = halos(step, part)
+            pl.when(has_up)(up.wait_send)
+            pl.when(has_down)(down.wait_send)
     for b in range(blocks):
         all_of(b, s1)
         all_of(b, s2)
@@ -247,7 +258,7 @@
     dma = pltpu.SemaphoreType.DMA
     return pl.pallas_call(
         kernel,
-        out_shape=jax.ShapeDtypeStruct(ensemble.shape, jnp.float32),
+        out_shape=pltpu.VMEM(ensemble.shape, jnp.float32),
         in_specs=[pl.BlockSpec(memory_space=pltpu.SMEM)] + [anywhere] * 5,
         out_specs=pl.BlockSpec(memory_space=pltpu.VMEM),
         scratch_shapes=[
@@ -259,7 +270,7 @@
             vmem(strip),
             vmem(strip), vmem(strip), vmem(strip), vmem(strip),
             dma((6,)), dma((blocks,)), dma((blocks,)), dma((blocks,)), dma((blocks,)),
-            dma((2 * ITERS,)), dma((2 * ITERS,)),
+            dma((2 * ITERS * PARTS,)), dma((2 * ITERS * PARTS,)),
         ],
         compiler_params=pltpu.CompilerParams(
             collective_id=0, has_side_effects=True, vmem_limit_bytes=60 << 20

time: 49.1 us -> 45 us (0.916)
  Pallas kernels: 46.8 us -> 44.1 us
  local copies, waits for them, and re-layouts: 1.87 us -> 0.8 us
    pallas_call x1, Pallas kernels: 46.8 us -> 44.1 us  [shards(): pl.pallas_call(kernel, out_shape=pltpu.VMEM(ensemble.shape, jnp.float32),...]
    unnamed x1, local copies, waits for them, and re-layouts: 1.87 us -> 0.8 us
where the time goes in v3:
time: 45 us; the launch traced here: 44.9 us
  Pallas kernels  44.1 us (98%)
  local copies, waits for them, and re-layouts  0.8 us (2%)
    pallas_call x1, Pallas kernels, shards(): pl.pallas_call(kernel, out_shape=pltpu.VMEM(ensemble.shape, jnp.float32),...  44.1 us

profile of v3, /device:TPU:32, one launch (start us, length us, event | category | flops | bytes accessed | tf_op | source)
XLA Modules:
  0.0 44.9 jit_solution(15097515887834220662)
XLA Ops:
  0.0 44.1 %shard_map.64 = f32[1,4,16,2048]{3,2,1,0:T(8,128)S(1)} custom-call(s32[32]{0:T(128)} %anc.1, f32[1,4,16,2048]{3,2,1,0:T(8,128)} %ens.1, f32[2,4,16,2048]{3,2,1,0:T(8,128)} %vel.1, f32[4,16,2048]{2,1,0:T(8,128)} %obs.1, f32[4,16,2048]{2,1,0:T(8,128)} %gain.1, f32[1,4,16,2048]{3,2,1,0:T(8,128)} %forc.1), custom_call_target="tpu_custom_call" | custom-call | tf_op jit(solution)/shard_map/pallas_call | solution.py:259
  44.1 0.8 %copy.8 = f32[1,4,16,2048]{3,2,1,0:T(8,128)} copy(f32[1,4,16,2048]{3,2,1,0:T(8,128)S(1)} %shard_map.64) | data formatting | bytes 1048576

commit v4 on v3

--- a/solution.py
+++ b/solution.py
@@ -11,7 +11,7 @@
 MESH = pl.DeviceIdType.MESH
 LANES = 128
 GROUP = 4
-PARTS = 2
+PARTS = 4
 TILE = 8
 
 
@@ -61,28 +61,45 @@
             state[k, pl.ds(l, rows, stride=levels), :] = raw[0, l, :, LANES * k : LANES * (k + 1)]
 
     def piece(j, b, top):
-        pair = b + (j // per_pair) * (pairs - 1 - 2 * b)
-        return (j % per_pair, pl.ds(pl.multiple_of(top + pair * TILE, TILE), TILE))
+        pair = b + (j % 2) * (pairs - 1 - 2 * b)
+        return (j // 2, pl.ds(pl.multiple_of(top + pair * TILE, TILE), TILE))
+
+    outer_is_up = t < tiles // 2
+
+    def inner_first(r):
+        side = jnp.where(outer_is_up, 1, 0)
+        side = side + (r // per_pair) * (1 - 2 * side)
+        return (me // 2 + (r % 4) * 4 + r % per_pair // 4) % per_pair * 2 + side
 
     def scatter(b):
         def send(r, carry):
-            j = partner(r)
-            pltpu.make_async_remote_copy(
+            j = inner_first(r)
+            copy = pltpu.make_async_remote_copy(
                 src_ref=state.at[piece(j, b, 0)],
                 dst_ref=inboxes[b].at[me],
                 send_sem=s1.at[b],
                 recv_sem=r1.at[b],
                 device_id={"particle": j},
                 device_id_type=MESH,
-            ).start()
+            )
+            pl.when(j != me)(copy.start)
             return carry
 
-        lax.fori_loop(1, n, send, 0)
+        lax.fori_loop(0, n, send, 0)
         inboxes[b][me] = state[piece(me, b, 0)]
 
     def all_of(b, sem):
         whole = inboxes[b].at[pl.ds(0, n - 1)]
         pltpu.make_async_copy(whole, whole, sem.at[b]).wait()
+
+    def arrived(b):
+        whole = inboxes[b].at[pl.ds(0, n - 1)]
+        pltpu.make_async_copy(whole, whole, r2.at[b + 1]).wait()
+
+    def side_arrived(side):
+        for own in (0, 1):
+            some = inboxes[0].at[pl.ds(0, per_pair - own)]
+            pl.when((me % 2 == side) == (own == 1))(pltpu.make_async_copy(some, some, r2.at[side]).wait)
 
     def deliver(b):
         all_of(b, r1)
@@ -95,7 +112,7 @@
                 src_ref=outbox.at[b, p],
                 dst_ref=fields[0].at[piece(me, b, TILE)],
                 send_sem=s2.at[b],
-                recv_sem=r2.at[b],
+                recv_sem=r2.at[me % 2 if b == 0 else b + 1],
                 device_id={"particle": p},
                 device_id_type=MESH,
             ).start()
@@ -104,33 +121,41 @@
         lax.fori_loop(1, n, send, 0)
         fields[0][piece(me, b, TILE)] = outbox[b, me]
 
-    def halos(step, part):
+    def halo(step, part, is_up):
         u = fields[step]
+        c = pl.ds(part * (strips // PARTS), strips // PARTS)
         sem = 2 * (PARTS * step + part)
+        mine = jnp.where(is_up, TILE, TILE * pairs)
+        there = jnp.where(is_up, TILE * (pairs + 1), 0)
+        return pltpu.make_async_remote_copy(
+            src_ref=u.at[c, pl.ds(pl.multiple_of(mine, TILE), TILE)],
+            dst_ref=u.at[c, pl.ds(pl.multiple_of(there, TILE), TILE)],
+            send_sem=hs.at[sem + jnp.where(is_up, 0, 1)],
+            recv_sem=hr.at[sem + jnp.where(is_up, 0, 1)],
+            device_id={"tile": jnp.where(is_up, t - 1, t + 1)},
+            device_id_type=MESH,
+        )
+
+    def arrival(step, part, is_up):
         c = pl.ds(part * (strips // PARTS), strips // PARTS)
-        up = pltpu.make_async_remote_copy(
-            src_ref=u.at[c, pl.ds(TILE, TILE)],
-            dst_ref=u.at[c, pl.ds(TILE * (pairs + 1), TILE)],
-            send_sem=hs.at[sem], recv_sem=hr.at[sem],
-            device_id={"tile": t - 1}, device_id_type=MESH,
-        )
-        down = pltpu.make_async_remote_copy(
-            src_ref=u.at[c, pl.ds(TILE * pairs, TILE)],
-            dst_ref=u.at[c, pl.ds(0, TILE)],
-            send_sem=hs.at[sem + 1], recv_sem=hr.at[sem + 1],
-            device_id={"tile": t + 1}, device_id_type=MESH,
-        )
-        return up, down
-
-    def send_halos(step, part):
-        up, down = halos(step, part)
-        pl.when(has_up)(up.start)
-        pl.when(has_down)(down.start)
-
-    def wait_halos(step, part):
-        up, down = halos(step, part)
-        pl.when(has_up)(down.wait_recv)
-        pl.when(has_down)(up.wait_recv)
+        rows_here = pl.ds(pl.multiple_of(jnp.where(is_up, 0, TILE * (pairs + 1)), TILE), TILE)
+        region = fields[step].at[c, rows_here]
+        return pltpu.make_async_copy(region, region, hr.at[2 * (PARTS * step + part) + jnp.where(is_up, 1, 0)])
+
+    sides = (outer_is_up, jnp.logical_not(outer_is_up))
+
+    def has(is_up):
+        return jnp.where(is_up, t > 0, t < tiles - 1)
+
+    def send_halos(step, part, is_up):
+        pl.when(has(is_up))(halo(step, part, is_up).start)
+
+    def edge(step, part, is_up):
+        pl.when(has(is_up))(arrival(step, part, is_up).wait)
+        pl.when(is_up)(lambda: advance(step, (0,), part, PARTS))
+        pl.when(jnp.logical_not(is_up))(lambda: advance(step, (pairs - 1,), part, PARTS))
+        if step < ITERS - 1:
+            send_halos(step + 1, part, is_up)
 
     def advance(step, some, part=0, parts=1):
         u = fields[step]
@@ -183,7 +208,6 @@
     scatter(0)
     scatter(1)
     scatter(2)
-
     for u in fields:
 
         @pl.when(jnp.logical_not(has_up))
@@ -206,42 +230,41 @@
             keep[k, r, :] = 0.4 - raw[3, l, :, c]
             add[k, r, :] = raw[3, l, :, c] * raw[4, l, :, c] + raw[5, l, :, c]
 
-    edges = (0, pairs - 1)
     deliver(0)
     scatter(3)
     deliver(1)
+    side_arrived(jnp.where(outer_is_up, 1, 0))
+    for part in range(PARTS):
+        send_halos(0, part, sides[1])
     deliver(2)
-    all_of(0, r2)
+    side_arrived(jnp.where(outer_is_up, 0, 1))
     for part in range(PARTS):
-        send_halos(0, part)
+        send_halos(0, part, sides[0])
     deliver(3)
-    all_of(1, r2)
-    for part in range(PARTS):
-        wait_halos(0, part)
-        advance(0, edges, part, PARTS)
-        send_halos(1, part)
-    all_of(2, r2)
+    arrived(1)
+    for side in sides:
+        for part in range(PARTS):
+            edge(0, part, side)
+    arrived(2)
     advance(0, (1, pairs - 2))
-    for part in range(PARTS):
-        wait_halos(1, part)
-        advance(1, edges, part, PARTS)
-        send_halos(2, part)
-    all_of(3, r2)
+    for side in sides:
+        for part in range(PARTS):
+            edge(1, part, side)
+    arrived(3)
     advance(0, range(2, pairs - 2))
     advance(1, range(1, pairs - 1))
     advance(2, range(1, pairs - 1))
-    for part in range(PARTS):
-        wait_halos(2, part)
-        advance(2, edges, part, PARTS)
+    for side in sides:
+        for part in range(PARTS):
+            edge(2, part, side)
     for k in range(strips):
         for l in range(levels):
             out[0, l, :, LANES * k : LANES * (k + 1)] = last[k, pl.ds(l, rows, stride=levels), :]
 
     for step in range(ITERS):
         for part in range(PARTS):
-            up, down = halos(step, part)
-            pl.when(has_up)(up.wait_send)
-            pl.when(has_down)(down.wait_send)
+            for side in sides:
+                pl.when(has(side))(halo(step, part, side).wait_send)
     for b in range(blocks):
         all_of(b, s1)
         all_of(b, s2)
@@ -269,7 +292,7 @@
             [vmem(padded)] * ITERS,
             vmem(strip),
             vmem(strip), vmem(strip), vmem(strip), vmem(strip),
-            dma((6,)), dma((blocks,)), dma((blocks,)), dma((blocks,)), dma((blocks,)),
+            dma((6,)), dma((blocks,)), dma((blocks,)), dma((blocks,)), dma((blocks + 1,)),
             dma((2 * ITERS * PARTS,)), dma((2 * ITERS * PARTS,)),
         ],
         compiler_params=pltpu.CompilerParams(

time: 45 us -> 44.4 us (0.987)
  Pallas kernels: 44.1 us -> 43.1 us
    pallas_call x1, Pallas kernels: 44.1 us -> 43.1 us  [shards(): pl.pallas_call(kernel, out_shape=pltpu.VMEM(ensemble.shape, jnp.float32),...]
where the time goes in v4:
time: 44.4 us; the launch traced here: 43.9 us
  Pallas kernels  43.1 us (97%)
  local copies, waits for them, and re-layouts  0.8 us (2%)
    pallas_call x1, Pallas kernels, shards(): pl.pallas_call(kernel, out_shape=pltpu.VMEM(ensemble.shape, jnp.float32),...  43.1 us

profile of v4, /device:TPU:32, one launch (start us, length us, event | category | flops | bytes accessed | tf_op | source)
XLA Modules:
  0.0 43.9 jit_solution(296120587146811665)
XLA Ops:
  0.0 43.1 %shard_map.64 = f32[1,4,16,2048]{3,2,1,0:T(8,128)S(1)} custom-call(s32[32]{0:T(128)} %anc.1, f32[1,4,16,2048]{3,2,1,0:T(8,128)} %ens.1, f32[2,4,16,2048]{3,2,1,0:T(8,128)} %vel.1, f32[4,16,2048]{2,1,0:T(8,128)} %obs.1, f32[4,16,2048]{2,1,0:T(8,128)} %gain.1, f32[1,4,16,2048]{3,2,1,0:T(8,128)} %forc.1), custom_call_target="tpu_custom_call" | custom-call | tf_op jit(solution)/shard_map/pallas_call | solution.py:282
  43.1 0.8 %copy.8 = f32[1,4,16,2048]{3,2,1,0:T(8,128)} copy(f32[1,4,16,2048]{3,2,1,0:T(8,128)S(1)} %shard_map.64) | data formatting | bytes 1048576

commit v5 on v4

--- a/solution.py
+++ b/solution.py
@@ -159,12 +159,13 @@
 
     def advance(step, some, part=0, parts=1):
         u = fields[step]
+        size = GROUP if parts > 1 else 4 * GROUP
 
         def group(i, carry):
             level = lax.broadcasted_iota(jnp.int32, (TILE, LANES), 0) % levels
             lane = lax.broadcasted_iota(jnp.int32, (TILE, LANES), 1)
-            first = i * GROUP
-            ks = [(first + strips - 1) % strips] + [first + k for k in range(GROUP)] + [(first + GROUP) % strips]
+            first = i * size
+            ks = [(first + strips - 1) % strips] + [first + k for k in range(size)] + [(first + size) % strips]
             for pair in some:
                 top = TILE * (pair + 1)
                 r = pl.ds(TILE * pair, TILE)
@@ -173,7 +174,7 @@
                 left2 = [pltpu.roll(x, LANES - 2, 1) for x in row[1:]]
                 right = [pltpu.roll(x, 1, 1) for x in row[:-1]]
                 right2 = [pltpu.roll(x, 2, 1) for x in row[:-1]]
-                for g in range(GROUP):
+                for g in range(size):
                     k = first + g
                     here = row[g + 1]
                     east = jnp.where(lane < LANES - 1, left[g], left[g + 1])
@@ -200,7 +201,7 @@
                         fields[step + 1][k, top : top + TILE, :] = value
             return carry
 
-        groups = strips // GROUP // parts
+        groups = strips // size // parts
         lax.fori_loop(part * groups, (part + 1) * groups, group, 0)
 
     pl.semaphore_wait(barrier, n - 1 + jnp.where(has_up, 1, 0) + jnp.where(has_down, 1, 0))

time: 44.4 us -> 44.4 us (level)
  no operation moved by 1% of the time
where the time goes in v5:
time: 44.4 us; the launch traced here: 43.6 us
  Pallas kernels  42.8 us (96%)
  local copies, waits for them, and re-layouts  0.8 us (2%)
    pallas_call x1, Pallas kernels, shards(): pl.pallas_call(kernel, out_shape=pltpu.VMEM(ensemble.shape, jnp.float32),...  42.8 us

profile of v5, /device:TPU:32, one launch (start us, length us, event | category | flops | bytes accessed | tf_op | source)
XLA Modules:
  0.0 43.6 jit_solution(1621118990903170879)
XLA Ops:
  0.0 42.8 %shard_map.64 = f32[1,4,16,2048]{3,2,1,0:T(8,128)S(1)} custom-call(s32[32]{0:T(128)} %anc.1, f32[1,4,16,2048]{3,2,1,0:T(8,128)} %ens.1, f32[2,4,16,2048]{3,2,1,0:T(8,128)} %vel.1, f32[4,16,2048]{2,1,0:T(8,128)} %obs.1, f32[4,16,2048]{2,1,0:T(8,128)} %gain.1, f32[1,4,16,2048]{3,2,1,0:T(8,128)} %forc.1), custom_call_target="tpu_custom_call" | custom-call | tf_op jit(solution)/shard_map/pallas_call | solution.py:283
  42.8 0.8 %copy.8 = f32[1,4,16,2048]{3,2,1,0:T(8,128)} copy(f32[1,4,16,2048]{3,2,1,0:T(8,128)S(1)} %shard_map.64) | data formatting | bytes 1048576

commit v6 on v5

--- a/solution.py
+++ b/solution.py
@@ -150,10 +150,23 @@
     def send_halos(step, part, is_up):
         pl.when(has(is_up))(halo(step, part, is_up).start)
 
+    def finish(part, half):
+        some = rows // 2
+        for k in range(part * (strips // PARTS), (part + 1) * (strips // PARTS)):
+            for l in range(levels):
+                out[0, l, some * half : some * (half + 1), LANES * k : LANES * (k + 1)] = last[
+                    k, pl.ds(some * levels * half + l, some, stride=levels), :
+                ]
+
     def edge(step, part, is_up):
         pl.when(has(is_up))(arrival(step, part, is_up).wait)
-        pl.when(is_up)(lambda: advance(step, (0,), part, PARTS))
-        pl.when(jnp.logical_not(is_up))(lambda: advance(step, (pairs - 1,), part, PARTS))
+        def side_step(pair, half):
+            advance(step, (pair,), part, PARTS)
+            if step == ITERS - 1:
+                finish(part, half)
+
+        pl.when(is_up)(lambda: side_step(0, 0))
+        pl.when(jnp.logical_not(is_up))(lambda: side_step(pairs - 1, 1))
         if step < ITERS - 1:
             send_halos(step + 1, part, is_up)
 
@@ -258,9 +271,6 @@
     for side in sides:
         for part in range(PARTS):
             edge(2, part, side)
-    for k in range(strips):
-        for l in range(levels):
-            out[0, l, :, LANES * k : LANES * (k + 1)] = last[k, pl.ds(l, rows, stride=levels), :]
 
     for step in range(ITERS):
         for part in range(PARTS):

time: 44.4 us -> 44.3 us (level)
  no operation moved by 1% of the time
where the time goes in v6:
time: 44.3 us; the launch traced here: 43.5 us
  Pallas kernels  42.7 us (96%)
  local copies, waits for them, and re-layouts  0.8 us (2%)
    pallas_call x1, Pallas kernels, shards(): pl.pallas_call(kernel, out_shape=pltpu.VMEM(ensemble.shape, jnp.float32),...  42.7 us

profile of v6, /device:TPU:32, one launch (start us, length us, event | category | flops | bytes accessed | tf_op | source)
XLA Modules:
  0.0 43.5 jit_solution(7847094348218194524)
XLA Ops:
  0.0 42.7 %shard_map.64 = f32[1,4,16,2048]{3,2,1,0:T(8,128)S(1)} custom-call(s32[32]{0:T(128)} %anc.1, f32[1,4,16,2048]{3,2,1,0:T(8,128)} %ens.1, f32[2,4,16,2048]{3,2,1,0:T(8,128)} %vel.1, f32[4,16,2048]{2,1,0:T(8,128)} %obs.1, f32[4,16,2048]{2,1,0:T(8,128)} %gain.1, f32[1,4,16,2048]{3,2,1,0:T(8,128)} %forc.1), custom_call_target="tpu_custom_call" | custom-call | tf_op jit(solution)/shard_map/pallas_call | solution.py:293
  42.7 0.8 %copy.8 = f32[1,4,16,2048]{3,2,1,0:T(8,128)} copy(f32[1,4,16,2048]{3,2,1,0:T(8,128)S(1)} %shard_map.64) | data formatting | bytes 1048576
